TPU v7x, 32 devices: a whole 2x2x4 slice. The times are simulated.
32 devices in a mesh: groups: 2 (over y), seq: 8 (over z, x), tp: 2 (over core).
Axes of the slice: x: 2, y: 2, z: 4, core: 2. Of those that a mesh axis runs over, the one named last changes fastest.
Arguments:
- features: bfloat16 [3, 4096, 4096], P(None, 'tp', ('groups', 'seq')), parts along dimension 2, may hold values from -6 to 6
- short_filter: float32 [3, 3, 4096], P(None, None, 'tp'), may hold values from -3.5 to 3.5
- mr_filter: bfloat16 [256, 128], P('tp'), may hold values from -0.5 to 0.5
- mr_bias: float32 [4096], P('tp'), may hold values from -4 to 4
- candidate: int32 [4096], P(('groups', 'seq')), parts along dimension 0, may hold values from 0 to 3, never falling along the last dimension, each value on 1 to 1024 neighbouring positions
Outputs:
- running: bfloat16 [4096, 4096], P('tp', ('groups', 'seq')), parts along dimension 1
There are 2 independent parts, one for each index of `groups`. A program takes and returns all parts, laid end to end along the dimension named above; an argument that names none is the same for every part. Nothing has to cross between parts.
Inputs may be any that keep to these rules, and one draw needn't show every extreme that they name: `candidate`: ids never fall along the stretch; every one of the 4 candidates has 1 to 1024 tokens, and one has exactly 1024.
All inputs are finite; a program needn't handle non-finite values.
Results may differ from a plain program's by a relative error of at most 0.009.
Values may be sent and summed in bfloat16 or wider, within the bound.
A program may use at most 128 MiB of HBM per device.

v0:
```python
import jax
import jax.numpy as jnp
from jax import lax
from jax.sharding import PartitionSpec as P

NCAND = 4


def passed_along(value, axis, steps):
    count = lax.axis_size(axis)
    initial, last = (max(0, -steps), min(count, count - steps))
    return lax.ppermute(value, axis, [(source, source + steps) for source in range(initial, last)])


def prefix(value, axis, join, neutral):
    count, mine = (lax.axis_size(axis), lax.axis_index(axis))
    pieces = jax.tree.map(lambda part: lax.all_gather(part, axis), value)
    running = jax.tree.map(
        lambda part, zero: jnp.full_like(part, 0) + jnp.asarray(zero, part.dtype), value, neutral
    )

    def lap(position, running):
        longer = join(running, jax.tree.map(lambda part: part[position], pieces))
        return jax.tree.map(lambda new, old: jnp.where(position < mine, new, old), longer, running)

    return lax.fori_loop(0, count - 1, lap, running)


def short_conv(window, ids_window, short_taps):
    near_same = (ids_window[1:-1] == ids_window[2:]).astype(jnp.float32)
    far_same = (ids_window[:-2] == ids_window[2:]).astype(jnp.float32)
    return (
        short_taps[0][:, :, None] * window[:, :, 2:]
        + short_taps[1][:, :, None] * (window[:, :, 1:-1] * near_same)
        + short_taps[2][:, :, None] * (window[:, :, :-2] * far_same)
    )


def add_pair(earlier, later):
    return (earlier[0] + later[0], earlier[1] + later[1])


def on_device(features, short_filter, mr_filter, mr_bias, candidate):
    channels = features.shape[1]
    tokens_here = features.shape[2]
    filter_len = mr_filter.shape[1]
    groups_here = mr_filter.shape[0]
    group_size = channels // groups_here
    rim_rows, prev_ids = passed_along(
        (features[:, :, -2:], candidate[-(filter_len - 1) :].astype(jnp.bfloat16)), "seq", 1
    )
    tail_ids = prev_ids.astype(jnp.int32)
    window = jnp.concatenate([rim_rows, features], axis=2).astype(jnp.float32)
    near_ids = jnp.concatenate([tail_ids[-2:], candidate])
    short_out = short_conv(window, near_ids, short_filter)
    gated = (short_out[1] * short_out[2]).astype(jnp.bfloat16)
    gate_tail = passed_along(gated[:, -(filter_len - 1) :], "seq", 1)
    extended = jnp.concatenate([gate_tail, gated], axis=1)
    extended_ids = jnp.concatenate([tail_ids, candidate])
    block_len = 128
    span_len = block_len + filter_len - 1
    lag_table = (
        lax.broadcasted_iota(jnp.int32, (span_len, block_len), 1)
        + (filter_len - 1)
        - lax.broadcasted_iota(jnp.int32, (span_len, block_len), 0)
    )
    picker = (
        lag_table[None] == lax.broadcasted_iota(jnp.int32, (filter_len, span_len, block_len), 0)
    ).astype(jnp.bfloat16)
    toeplitz = jnp.dot(
        mr_filter,
        picker.reshape(filter_len, span_len * block_len),
        preferred_element_type=jnp.bfloat16,
    ).reshape(groups_here, span_len, block_len)

    def conv_block(block_index, conv_acc):
        block_start = block_index * block_len
        key_rows = lax.dynamic_slice_in_dim(extended, block_start, span_len, 1).reshape(
            groups_here, group_size, span_len
        )
        key_ids = lax.dynamic_slice_in_dim(extended_ids, block_start, span_len, 0)
        out_ids = lax.dynamic_slice_in_dim(candidate, block_start, block_len, 0)
        masked = toeplitz * (key_ids[:, None] == out_ids[None, :]).astype(jnp.bfloat16)[None]
        block_out = jnp.einsum("gsk,gkt->gst", key_rows, masked, preferred_element_type=jnp.float32)
        return lax.dynamic_update_slice_in_dim(
            conv_acc, block_out.reshape(channels, block_len), block_start, 1
        )

    conv = lax.fori_loop(
        0, tokens_here // block_len, conv_block, jnp.zeros((channels, tokens_here), jnp.float32)
    )
    gated_f = gated.astype(jnp.float32)
    mixed = (short_out[0] * (conv + mr_bias[:, None] * gated_f)).astype(jnp.bfloat16)
    member = candidate[:, None] == lax.broadcasted_iota(jnp.int32, (tokens_here, NCAND), 1)
    partial_sum = jnp.dot(mixed, member.astype(jnp.bfloat16), preferred_element_type=jnp.float32)
    partial_count = jnp.sum(member.astype(jnp.float32), axis=0)
    causal_same = (
        lax.broadcasted_iota(jnp.int32, (tokens_here, tokens_here), 0)
        <= lax.broadcasted_iota(jnp.int32, (tokens_here, tokens_here), 1)
    ) & (candidate[:, None] == candidate[None, :])
    local_sum = jnp.dot(mixed, causal_same.astype(jnp.bfloat16), preferred_element_type=jnp.float32)
    local_count = jnp.sum(causal_same.astype(jnp.float32), axis=0)
    earlier_sum, earlier_count = prefix(
        (partial_sum, partial_count),
        "seq",
        add_pair,
        (jnp.zeros_like(partial_sum), jnp.zeros_like(partial_count)),
    )
    member_rows = (
        lax.broadcasted_iota(jnp.int32, (NCAND, tokens_here), 0) == candidate[None, :]
    ).astype(jnp.float32)
    before = jnp.dot(earlier_sum, member_rows, precision=lax.Precision.HIGHEST)
    count_before = jnp.dot(earlier_count, member_rows, precision=lax.Precision.HIGHEST)
    return ((before + local_sum) / jnp.sqrt(count_before + local_count)[None, :]).astype(
        jnp.bfloat16
    )


def solution(mesh):
    placed = (
        P(None, "tp", ("groups", "seq")),
        P(None, None, "tp"),
        P("tp", None),
        P("tp"),
        P(("groups", "seq")),
    )
    return jax.shard_map(
        on_device, mesh=mesh, in_specs=placed, out_specs=P("tp", ("groups", "seq")), check_vma=False
    )
```

profile of v0, /device:TPU:0, one launch (start us, length us, event | category | flops | bytes accessed | tf_op | source)
XLA Modules:
  0.0 126.9 jit_solution(5900662474866181793)
XLA Ops:
  0.0 0.9 convert.3
  0.9 5.0 %collective-permute-start.1 = (bf16[127]{0:T(256)(128)(2,1)S(1)}, bf16[127]{0:T(256)(128)(2,1)S(1)}, u32[]{:S(2)}, u32[]{:S(2)}) collective-permute-start(bf16[127]{0:T(256)(128)(2,1)S(1)} %slice.51), channel_id=1, source_target_pairs={{0,2},{2,4},{4,6},{6,8},{8,10},{10,12},{12,14},{1,3},{3,5},{5,7},{... | collective-permute-start | bytes 770 | tf_op jit(solution)/shard_map/ppermute | solution.py:12
  5.9 3.1 %slice.47 = bf16[3,2048,2]{2,1,0:T(8,128)(2,1)} slice(bf16[3,2048,256]{2,1,0:T(8,128)(2,1)} %param.9), slice={[0:3], [0:2048], [254:256]} | slice | bytes 49152 | tf_op jit(solution)/shard_map/slice | solution.py:50
  9.0 1.7 %copy.18 = bf16[3,2048,2]{1,2,0:T(2,128)(2,1)S(1)} copy(bf16[3,2048,2]{2,1,0:T(8,128)(2,1)} %slice.47) | data formatting | bytes 49152
  10.7 4.1 %collective-permute-start = (bf16[3,2048,2]{1,2,0:T(2,128)(2,1)S(1)}, bf16[3,2048,2]{1,2,0:T(2,128)(2,1)}, u32[]{:S(2)}, u32[]{:S(2)}) collective-permute-start(bf16[3,2048,2]{1,2,0:T(2,128)(2,1)S(1)} %copy.18), channel_id=1, source_target_pairs={{0,2},{2,4},{4,6},{6,8},{8,10},{10,12},{12,14},{1,3},{3,5},{5,7},{... | collective-permute-start | bytes 73736 | tf_op jit(solution)/shard_map/ppermute | solution.py:12
  15.1 0.6 collective-permute-done
  15.7 2.3 %copy.15 = bf16[3,2048,2]{2,1,0:T(8,128)(2,1)} copy(bf16[3,2048,2]{1,2,0:T(2,128)(2,1)} %collective-permute-done) | data formatting | bytes 49152 | tf_op jit(solution)/shard_map/ppermute | solution.py:12
  18.0 3.3 %maximum_convert_fusion = f32[3,2048,258]{2,1,0:T(8,128)S(1)} fusion(bf16[3,2048,256]{2,1,0:T(8,128)(2,1)S(1)} %copy-done.2, bf16[3,2048,2]{2,1,0:T(8,128)(2,1)} %copy.15), kind=kLoop, calls=%fused_computation.20 | loop fusion | flops 6340608 | bytes 9510912 | tf_op jit(solution)/shard_map/convert_element_type | solution.py:53
  21.3 6.3 %fusion.7 = f32[3,2048,256]{2,1,0:T(8,128)S(1)} fusion(f32[3,2048,258]{2,1,0:T(8,128)S(1)} %maximum_convert_fusion, f32[256]{0:T(256)S(1)} %get-tuple-element.324, f32[3,2048]{1,0:T(4,128)S(1)} %get-tuple-element.321, f32[256]{0:T(256)S(1)} %get-tuple-element.323, f32[3,2048]{1,0:T(4,128)S(1)} %get-tuple-element.322, f32[3,2048]{1,0:T(4,128)S(1)} %get-tuple-element.320), kind=kLoop, calls=%fused_computation.15 | loop fusion | flops 11010048 | bytes 25241600 | tf_op jit(solution)/shard_map/add | solution.py:33
  27.6 2.6 %copy-done.1 = f32[3,2048,256]{2,1,0:T(8,128)} copy-done((f32[3,2048,256]{2,1,0:T(8,128)}, f32[3,2048,256]{2,1,0:T(8,128)S(1)}, u32[]{:S(2)}) %copy-start.1) | copy-done | bytes 6291480
  30.2 0.2 fusion.15
  30.4 0.2 slice.67
  30.6 5.1 %collective-permute-start.2 = (bf16[2048,127]{1,0:T(8,128)(2,1)S(1)}, bf16[2048,127]{1,0:T(8,128)(2,1)}, u32[]{:S(2)}, u32[]{:S(2)}) collective-permute-start(bf16[2048,127]{1,0:T(8,128)(2,1)S(1)} %slice.67), channel_id=1, source_target_pairs={{0,2},{2,4},{4,6},{6,8},{8,10},{10,12},{12,14},{1,3},{3,5},{5,7},{... | collective-permute-start | bytes 1560584 | tf_op jit(solution)/shard_map/ppermute | solution.py:12
  35.8 4.5 %convolution_convert_fusion = bf16[32640,128]{1,0:T(8,128)(2,1)} fusion(bf16[128,128]{1,0:T(8,128)(2,1)S(1)} %copy-done, s32[32640]{0:T(1024)S(1)} %subtract_bitcast_fusion), kind=kOutput, calls=%fused_computation.9 | convolution fusion | flops 1082081280 | bytes 8519168
  40.3 11.8 %copy.16 = bf16[128,255,128]{2,1,0:T(8,128)(2,1)} copy(bf16[128,255,128]{0,2,1:T(8,128)(2,1)} %bitcast.50) | data formatting | bytes 16711680 | tf_op jit(solution)/shard_map/while | solution.py:89
  52.1 0.6 dynamic-slice
  53.5 0.2 dynamic-update-slice
  53.8 19.0 %all-reduce = f32[32]{0:T(128)S(1)} all-reduce(f32[32]{0:T(128)S(1)} %dynamic-update-slice), channel_id=3, replica_groups=mesh['groups'=2,'seq'=8,'tp'=2] {'seq'}, use_global_device_ids=true, to_apply=%add | all-reduce | flops 32 | bytes 256
  72.8 0.1 convert_reduce_fusion
  73.0 1.8 %pad_maximum_fusion = bf16[2048,383]{1,0:T(8,128)(2,1)S(1)} fusion(bf16[2048,256]{1,0:T(8,128)(2,1)S(1)} %fusion.15, bf16[2048,127]{1,0:T(8,128)(2,1)} %collective-permute-done.2), kind=kLoop, calls=%fused_computation.29 | loop fusion | flops 3137536 | bytes 3137536 | tf_op jit(solution)/shard_map/concatenate | solution.py:58
  74.8 1.5 %broadcast_in_dim.14 = f32[2048,256]{1,0:T(8,128)} broadcast(f32[]{:T(128)} %constant.67.clone.1), dimensions={} | broadcast | bytes 2097156 | tf_op jit(solution)/shard_map/broadcast_in_dim | solution.py:90
  76.3 12.3 %while.29 = (s32[]{:T(128)}, f32[2048,256]{1,0:T(8,128)}, bf16[2048,383]{1,0:T(8,128)(2,1)S(1)}, s32[383]{0:T(512)S(1)}, s32[256]{0:T(256)S(1)}, /*index=5*/bf16...) while((s32[]{:T(128)}, f32[2048,256]{1,0:T(8,128)}, ...), condition=%wide.region_1.0_spmd, body=%wide.region_0.0_spmd.sunk | while | flops 137936640 | bytes 14770360 | solution.py:89
  76.6 4.7 %fusion.37 = f32[128,16,128]{2,1,0:T(8,128)S(1)} fusion(bf16[128,16,255]{2,1,0:T(8,128)(2,1)S(1)} %bitcast.49, bf16[128,255,128]{2,1,0:T(8,128)(2,1)} %get-tuple-element.426, bf16[255,128]{1,0:T(8,128)(2,1)S(1)} %compare_convert_fusion.4), kind=kOutput, calls=%fused_computation.clone.1 | convolution fusion | flops 137871360 | bytes 10514176 | tf_op jit(solution)/shard_map/while/body/eval_jaxpr/gsk,gkt->gst/dot_general | solution.py:84
  81.3 1.1 constant_dynamic-update-slice_fusion.2
  82.8 4.7 %fusion.37 = f32[128,16,128]{2,1,0:T(8,128)S(1)} fusion(bf16[128,16,255]{2,1,0:T(8,128)(2,1)S(1)} %bitcast.49, bf16[128,255,128]{2,1,0:T(8,128)(2,1)} %get-tuple-element.426, bf16[255,128]{1,0:T(8,128)(2,1)S(1)} %compare_convert_fusion.4), kind=kOutput, calls=%fused_computation.clone.1 | convolution fusion | flops 137871360 | bytes 10514176 | tf_op jit(solution)/shard_map/while/body/eval_jaxpr/gsk,gkt->gst/dot_general | solution.py:84
  87.5 1.1 constant_dynamic-update-slice_fusion.2
  88.6 3.9 %fusion.14 = bf16[2048,256]{1,0:T(8,128)(2,1)S(1)} fusion(f32[3,2048,256]{2,1,0:T(8,128)} %copy-done.1, f32[2048,256]{1,0:T(8,128)} %get-tuple-element.224, f32[2048]{0:T(1024)S(1)} %copy-done.5), kind=kLoop, calls=%fused_computation.28 | loop fusion | flops 3670016 | bytes 9445376 | tf_op jit(solution)/shard_map/convert_element_type | solution.py:93
  92.5 0.4 fusion.22
  92.8 0.5 fusion.17
  93.4 30.9 %all-gather = f32[16384,4]{0,1:T(4,128)S(1)} all-gather(f32[2048,4]{0,1:T(4,128)S(1)} %fusion.22), channel_id=2, replica_groups=mesh['groups'=2,'seq'=8,'tp'=2] {'seq'}, dimensions={0}, use_global_device_ids=true | all-gather | bytes 294912 | tf_op jit(solution)/shard_map/all_gather | solution.py:17
  124.2 0.5 while.30
  124.8 2.0 %fusion.11 = bf16[2048,256]{1,0:T(8,128)(2,1)} fusion(f32[2048,256]{1,0:T(8,128)S(1)} %fusion.17, f32[2048,4]{0,1:T(4,128)S(1)} %get-tuple-element.225, f32[256]{0:T(256)S(1)} %add_sqrt_fusion, s32[256]{0:T(256)S(1)} %get-tuple-element.457), kind=kOutput, calls=%fused_computation.23 | convolution fusion | flops 26739712 | bytes 3180544 | tf_op jit(solution)/shard_map/dot_general | solution.py:112
  (53 shorter events, 1.7 us)
Async XLA Ops:
  0.0 35.8 %copy-start = (bf16[128,128]{1,0:T(8,128)(2,1)S(1)}, bf16[128,128]{1,0:T(8,128)(2,1)}, u32[]{:S(2)}) copy-start(bf16[128,128]{1,0:T(8,128)(2,1)} %param.11) | copy-start | bytes 98308
  0.0 14.9 %copy-start.4 = (s32[256]{0:T(256)S(1)}, s32[256]{0:T(256)}, u32[]{:S(2)}) copy-start(s32[256]{0:T(256)} %param.13) | copy-start | bytes 3076
  0.0 17.9 %copy-start.2 = (bf16[3,2048,256]{2,1,0:T(8,128)(2,1)S(1)}, bf16[3,2048,256]{2,1,0:T(8,128)(2,1)}, u32[]{:S(2)}) copy-start(bf16[3,2048,256]{2,1,0:T(8,128)(2,1)} %param.9) | copy-start | bytes 9437188
  0.0 14.8 %copy-start.3 = (f32[3,3,2048]{2,1,0:T(4,128)S(1)}, f32[3,3,2048]{2,1,0:T(4,128)}, u32[]{:S(2)}) copy-start(f32[3,3,2048]{2,1,0:T(4,128)} %param.10) | copy-start | bytes 221188
  0.9 13.9 %collective-permute-start.1 = (bf16[127]{0:T(256)(128)(2,1)S(1)}, bf16[127]{0:T(256)(128)(2,1)S(1)}, u32[]{:S(2)}, u32[]{:S(2)}) collective-permute-start(bf16[127]{0:T(256)(128)(2,1)S(1)} %slice.51), channel_id=1, source_target_pairs={{0,2},{2,4},{4,6},{6,8},{8,10},{10,12},{12,14},{1,3},{3,5},{5,7},{... | collective-permute-start | bytes 770 | tf_op jit(solution)/shard_map/ppermute | solution.py:12
  10.7 5.0 %collective-permute-start = (bf16[3,2048,2]{1,2,0:T(2,128)(2,1)S(1)}, bf16[3,2048,2]{1,2,0:T(2,128)(2,1)}, u32[]{:S(2)}, u32[]{:S(2)}) collective-permute-start(bf16[3,2048,2]{1,2,0:T(2,128)(2,1)S(1)} %copy.18), channel_id=1, source_target_pairs={{0,2},{2,4},{4,6},{6,8},{8,10},{10,12},{12,14},{1,3},{3,5},{5,7},{... | collective-permute-start | bytes 73736 | tf_op jit(solution)/shard_map/ppermute | solution.py:12
  27.6 2.6 %copy-start.1 = (f32[3,2048,256]{2,1,0:T(8,128)}, f32[3,2048,256]{2,1,0:T(8,128)S(1)}, u32[]{:S(2)}) copy-start(f32[3,2048,256]{2,1,0:T(8,128)S(1)} %fusion.7) | copy-start | bytes 18874372
  30.6 42.3 %collective-permute-start.2 = (bf16[2048,127]{1,0:T(8,128)(2,1)S(1)}, bf16[2048,127]{1,0:T(8,128)(2,1)}, u32[]{:S(2)}, u32[]{:S(2)}) collective-permute-start(bf16[2048,127]{1,0:T(8,128)(2,1)S(1)} %slice.67), channel_id=1, source_target_pairs={{0,2},{2,4},{4,6},{6,8},{8,10},{10,12},{12,14},{1,3},{3,5},{5,7},{... | collective-permute-start | bytes 1560584 | tf_op jit(solution)/shard_map/ppermute | solution.py:12
  40.3 11.8 %copy-start.6 = (u32[32]{0:T(128)S(1)}, u32[32]{0:T(128)}, u32[]{:S(2)}) copy-start(u32[32]{0:T(128)} %constant.73) | copy-start | bytes 388
  76.3 12.3 %copy-start.5 = (f32[2048]{0:T(1024)S(1)}, f32[2048]{0:T(1024)}, u32[]{:S(2)}) copy-start(f32[2048]{0:T(1024)} %param.12) | copy-start | bytes 24580
where the time goes:
time: 128 us; the launch traced here: 127 us
  blocking collectives  49.8 us (39%)
  local copies, waits for them, and re-layouts  27.1 us (21%)
  other arithmetic  17.4 us (14%)
  matrix products  16.9 us (13%)
  starting transfers between devices  14.2 us (11%)
    all_gather x1, blocking collectives, prefix(): pieces = jax.tree.map(lambda part: lax.all_gather(part, axis), value)  30.9 us
    unnamed x1, blocking collectives  19 us
    ppermute x3, starting transfers between devices, passed_along(): lax.ppermute(value, axis, [(source, source + steps) for source in range(i...  14.2 us
    while x1, local copies, waits for them, and re-layouts, on_device(): lax.fori_loop(0, tokens_here // block_len, conv_block, jnp.zeros((channel...  11.8 us
    dot_general x2, matrix products, conv_block(): jnp.einsum('gsk,gkt->gst', key_rows, masked, preferred_element_type=jnp.f...  9.33 us
    add x1, other arithmetic, short_conv(): short_taps[0][:, :, None] * window[:, :, 2:]  6.32 us
    unnamed x18, local copies, waits for them, and re-layouts  5.26 us
    unnamed x1, matrix products  4.54 us
  transfers between devices with their start and end apart: 3, of which 1 were waited for; matrix products, arithmetic and copies ran while one was open for 18% of the time, Pallas kernels for 0%

commit v1 on v0

v1 whole, which is shorter than its diff:
```python
import functools

import jax
import jax.numpy as jnp
from jax import lax
from jax.experimental import pallas as pl
from jax.experimental.pallas import tpu as pltpu
from jax.sharding import PartitionSpec as P

NCAND = 4
ROWS = 128
LANES = 128
F32 = jnp.float32
BF16 = jnp.bfloat16


def iota(shape, dim):
    return lax.broadcasted_iota(jnp.int32, shape, dim)


def dot(a, b):
    return jnp.dot(a, b, preferred_element_type=F32)


def earlier_ids(ids, own):
    total = jnp.zeros(own.shape, jnp.int32)
    for cand in range(NCAND):
        fewer = jnp.sum((ids < cand).astype(F32), axis=1, keepdims=True).astype(jnp.int32)
        total = jnp.where(own == cand, fewer, total)
    return total


def kernel(
    count, reach,
    x_ref, filt_ref, mr_ref, bias_ref, cand_ref, out_ref,
    rows_ref, prm_ref, mrf_ref, shift_ref, band_ref, pool_ref, table_ref,
    g0_ref, g1_ref, gh_ref, gate_ref, conv_ref, mixsum_ref,
    rim_out, rim_in, ids_in, sums_out, sums_in,
    halo_send, halo_recv, rim_send, rim_recv, ids_send, ids_recv, sums_send, sums_recv,
):
    me = lax.axis_index("seq")
    channels, tokens = out_ref.shape
    chunks = channels // ROWS
    groups = mr_ref.shape[0]
    size = channels // groups
    per_chunk = ROWS // size
    n_to = jnp.minimum(reach, count - 1 - me)
    n_from = jnp.minimum(reach, me)

    def halo_copy(i):
        rows = pl.ds(pl.multiple_of(i * ROWS, ROWS), ROWS)
        return pltpu.make_async_remote_copy(
            src_ref=g1_ref.at[rows], dst_ref=gh_ref.at[rows],
            send_sem=halo_send.at[i], recv_sem=halo_recv.at[i],
            device_id={"seq": me + 1}, device_id_type=pl.DeviceIdType.MESH)

    def rim_copy():
        return pltpu.make_async_remote_copy(
            src_ref=rim_out, dst_ref=rim_in, send_sem=rim_send, recv_sem=rim_recv,
            device_id={"seq": me + 1}, device_id_type=pl.DeviceIdType.MESH)

    def ids_copy(d):
        return pltpu.make_async_remote_copy(
            src_ref=cand_ref, dst_ref=ids_in.at[d - 1],
            send_sem=ids_send.at[d - 1], recv_sem=ids_recv.at[d - 1],
            device_id={"seq": me + d}, device_id_type=pl.DeviceIdType.MESH)

    def sums_copy(d):
        return pltpu.make_async_remote_copy(
            src_ref=sums_out, dst_ref=sums_in.at[d - 1],
            send_sem=sums_send.at[d - 1], recv_sem=sums_recv.at[d - 1],
            device_id={"seq": me + d}, device_id_type=pl.DeviceIdType.MESH)

    def loop(low, high, body):
        def step(i, carry):
            body(i)
            return carry
        lax.fori_loop(low, high, step, 0)

    barrier = pltpu.get_barrier_semaphore()
    loop(1, n_from + 1, lambda d: pl.semaphore_signal(
        barrier, inc=1, device_id={"seq": me - d}, device_id_type=pl.DeviceIdType.MESH))

    own = cand_ref[...]
    start = earlier_ids(own, own)
    k2, t2 = iota((tokens, tokens), 0), iota((tokens, tokens), 1)
    inside = k2 >= start
    band_ref[...] = (inside & (k2 <= t2) & (t2 - k2 < LANES)).astype(F32).astype(BF16)
    pool_ref[...] = (inside & (k2 <= t2)).astype(F32).astype(BF16)
    shift_ref[0] = (inside & (k2 == t2 - 1)).astype(F32).astype(BF16)
    shift_ref[1] = (inside & (k2 == t2 - 2)).astype(F32).astype(BF16)

    row_k, lane_k = iota((16, LANES), 0), iota((16, LANES), 1)
    rim = jnp.zeros((16, channels), F32)
    for b in range(3):
        pick = (lane_k - (LANES - 2) == row_k - 2 * b) & (lane_k >= LANES - 2)
        rim = rim + lax.dot_general(
            pick.astype(F32).astype(BF16), x_ref[b, :, tokens - LANES:],
            (((1,), (1,)), ((), ())), preferred_element_type=F32)
    rim_out[...] = rim.astype(BF16)

    @pl.when(me + 1 < count)
    def _():
        pl.semaphore_wait(barrier, n_to)

    loop(1, n_to + 1, lambda d: ids_copy(d).start())

    @pl.when(me + 1 < count)
    def _():
        rim_copy().start()

    rows_ref[...] = jnp.zeros_like(rows_ref)

    def tail(i):
        rows = pl.ds(pl.multiple_of(i * ROWS, ROWS), ROWS)
        for j in range(3):
            rows_ref[3 * j:3 * j + 3, :] = filt_ref[j, :, rows]
        rows_ref[9:10, :] = bias_ref[:, rows]
        prm = rows_ref[...].T
        prm_ref[rows, :] = prm
        outs = []
        for b in (1, 2):
            x = x_ref[b, rows, :]
            one = dot(x, shift_ref[0, :, LANES:])
            two = dot(x, shift_ref[1, :, LANES:])
            outs.append(prm[:, b:b + 1] * x[:, LANES:].astype(F32)
                        + prm[:, 3 + b:4 + b] * one + prm[:, 6 + b:7 + b] * two)
        g1_ref[rows, :] = (outs[0] * outs[1]).astype(BF16)

        @pl.when(me + 1 < count)
        def _():
            halo_copy(i).start()

    loop(0, chunks, tail)
    mrf_ref[...] = mr_ref[...].astype(F32)

    @pl.when(me == 0)
    def _():
        gh_ref[...] = jnp.zeros_like(gh_ref)
        rim_in[...] = jnp.zeros_like(rim_in)
        ids_in[0] = jnp.full(ids_in.shape[1:], -1, jnp.int32)

    @pl.when(me > 0)
    def _():
        rim_copy().wait_recv()
    loop(1, n_from + 1, lambda d: ids_copy(d).wait_recv())

    start_all = start + earlier_ids(ids_in[0][:, tokens - LANES:], own) - LANES
    kh, th = iota((LANES, LANES), 0), iota((LANES, LANES), 1)
    halo_mask = ((kh > th) & (kh - LANES >= start_all[:, :LANES])).astype(F32).astype(BF16)
    row_q, lane_q = iota((16, LANES), 0), iota((16, LANES), 1)

    def rim_pick(b, lag):
        token = row_q - 2 * b - 2
        hit = (token == lane_q - lag) & (token >= start_all[:, :LANES]) & (token < 0) & (token >= -2)
        return hit.astype(F32).astype(BF16)

    picks = [[rim_pick(b, lag) for lag in (1, 2)] for b in range(3)]

    def head(i):
        rows = pl.ds(pl.multiple_of(i * ROWS, ROWS), ROWS)
        prm = prm_ref[rows, :]
        edge = rim_in[:, rows]
        outs = []
        for b in range(3):
            x = x_ref[b, rows, :]
            lags = [dot(x, shift_ref[j, :, :LANES]) + lax.dot_general(
                edge, picks[b][j], (((0,), (0,)), ((), ())), preferred_element_type=F32)
                for j in range(2)]
            outs.append(prm[:, b:b + 1] * x[:, :LANES].astype(F32)
                        + prm[:, 3 + b:4 + b] * lags[0] + prm[:, 6 + b:7 + b] * lags[1])
        g0_ref[rows, :] = (outs[1] * outs[2]).astype(BF16)
        gate_ref[rows, :LANES] = outs[0]
        x = x_ref[0, rows, :]
        one = dot(x, shift_ref[0, :, LANES:])
        two = dot(x, shift_ref[1, :, LANES:])
        gate_ref[rows, LANES:] = (prm[:, 0:1] * x[:, LANES:].astype(F32)
                                  + prm[:, 3:4] * one + prm[:, 6:7] * two)

    loop(0, chunks, head)

    def conv(i):
        for u in range(4):
            group = i * 4 + u
            rows = pl.ds(pl.multiple_of(group * size, size), size)
            taps = jnp.broadcast_to(mrf_ref[pl.ds(group, 1), :], (LANES, LANES))
            wheel = pltpu.roll(taps, 0, 1, stride=1, stride_axis=0).astype(BF16)
            table_ref[group] = wheel * halo_mask
            upper = jnp.concatenate([wheel, wheel], axis=1) * band_ref[:LANES, :]
            right = wheel * band_ref[LANES:, LANES:]
            near = dot(g0_ref[rows, :], upper)
            conv_ref[rows, :LANES] = near[:, :LANES]
            conv_ref[rows, LANES:] = near[:, LANES:] + dot(g1_ref[rows, :], right)

    loop(0, groups // 4, conv)

    last = jnp.max(own.astype(F32), axis=1, keepdims=True)
    last_of = (iota((tokens, tokens), 0) >= earlier_ids(own, last.astype(jnp.int32)))
    last_col = last_of[:, :LANES].astype(F32)
    lane_p = iota((tokens, LANES), 1)
    mixsum_ref[...] = jnp.zeros_like(mixsum_ref)

    def mix(i):
        rows = pl.ds(pl.multiple_of(i * ROWS, ROWS), ROWS)

        @pl.when(me > 0)
        def _():
            halo_copy(i).wait_recv()

        for u in range(per_chunk):
            group = i * per_chunk + u
            some = pl.ds(pl.multiple_of(group * size, size), size)
            conv_ref[some, :LANES] += dot(gh_ref[some, :], table_ref[group])
        bias = prm_ref[rows, 9:10]
        gated = jnp.concatenate([g0_ref[rows, :], g1_ref[rows, :]], axis=1).astype(F32)
        mixed = (gate_ref[rows, :] * (conv_ref[rows, :] + bias * gated)).astype(BF16)
        conv_ref[rows, :] = dot(mixed, pool_ref[...])
        mixsum_ref[...] += dot(mixed, jnp.where(lane_p == i, last_col, 0.0).astype(BF16))

    loop(0, chunks, mix)

    sums_out[...] = mixsum_ref[...].T[:sums_out.shape[0], :]
    loop(1, n_to + 1, lambda d: sums_copy(d).start())

    first = jnp.min(own.astype(F32), axis=1, keepdims=True).astype(jnp.int32)
    mixsum_ref[...] = jnp.zeros_like(mixsum_ref)

    def gather(d, before):
        sums_copy(d).wait_recv()
        ids = ids_in[d - 1]
        same = jnp.max(ids.astype(F32), axis=1, keepdims=True).astype(jnp.int32) == first
        mixsum_ref[:sums_out.shape[0], :] += jnp.where(same, sums_in[d - 1], 0.0)
        return before + jnp.sum((ids == first).astype(F32), axis=1, keepdims=True)

    before = lax.fori_loop(1, n_from + 1, gather, jnp.zeros((1, 1), F32))
    carried = (start == 0).astype(F32)
    seen = (iota(start.shape, 1) + 1 - start).astype(F32) + carried * before
    scale = 1.0 / jnp.sqrt(seen)
    mixsum_ref[...] = mixsum_ref[...].T

    def finish(i):
        rows = pl.ds(pl.multiple_of(i * ROWS, ROWS), ROWS)
        column = jnp.sum(jnp.where(iota((ROWS, LANES), 1) == i, mixsum_ref[...], 0.0), axis=1, keepdims=True)
        out_ref[rows, :] = ((conv_ref[rows, :] + column * carried) * scale).astype(BF16)

    loop(0, chunks, finish)

    loop(1, n_to + 1, lambda d: sums_copy(d).wait_send())
    loop(1, n_to + 1, lambda d: ids_copy(d).wait_send())

    @pl.when(me + 1 < count)
    def _():
        rim_copy().wait_send()
        loop(0, chunks, lambda i: halo_copy(i).wait_send())


def on_device(features, short_filter, mr_filter, mr_bias, candidate):
    count = lax.axis_size("seq")
    reach = max(1, count // 2)
    _, channels, tokens = features.shape
    groups = mr_filter.shape[0]
    chunks = channels // ROWS
    sum_rows = -(-chunks // 8) * 8
    dma = pltpu.SemaphoreType.DMA
    vmem = pl.BlockSpec(memory_space=pltpu.VMEM)
    return pl.pallas_call(
        functools.partial(kernel, count, reach),
        out_shape=jax.ShapeDtypeStruct((channels, tokens), BF16),
        in_specs=[vmem] * 5,
        out_specs=vmem,
        scratch_shapes=[
            pltpu.VMEM((ROWS, LANES), F32),
            pltpu.VMEM((channels, LANES), F32),
            pltpu.VMEM((groups, LANES), F32),
            pltpu.VMEM((2, tokens, tokens), BF16),
            pltpu.VMEM((tokens, tokens), BF16),
            pltpu.VMEM((tokens, tokens), BF16),
            pltpu.VMEM((groups, LANES, LANES), BF16),
            pltpu.VMEM((channels, LANES), BF16),
            pltpu.VMEM((channels, LANES), BF16),
            pltpu.VMEM((channels, LANES), BF16),
            pltpu.VMEM((channels, tokens), F32),
            pltpu.VMEM((channels, tokens), F32),
            pltpu.VMEM((LANES, LANES), F32),
            pltpu.VMEM((16, channels), BF16),
            pltpu.VMEM((16, channels), BF16),
            pltpu.VMEM((reach, 1, tokens), jnp.int32),
            pltpu.VMEM((sum_rows, LANES), F32),
            pltpu.VMEM((reach, sum_rows, LANES), F32),
            dma((chunks,)), dma((chunks,)), dma, dma,
            dma((reach,)), dma((reach,)), dma((reach,)), dma((reach,)),
        ],
        compiler_params=pltpu.CompilerParams(
            collective_id=0, has_side_effects=True, vmem_limit_bytes=48 << 20),
        cost_estimate=pl.CostEstimate(
            flops=2 * channels * tokens * 1500, bytes_accessed=8 * channels * tokens, transcendentals=0),
    )(features, short_filter, mr_filter, mr_bias[None, :], candidate[None, :])


def solution(mesh):
    placed = (
        P(None, "tp", ("groups", "seq")),
        P(None, None, "tp"),
        P("tp", None),
        P("tp"),
        P(("groups", "seq")),
    )
    return jax.shard_map(
        on_device, mesh=mesh, in_specs=placed, out_specs=P("tp", ("groups", "seq")), check_vma=False
    )
```

time: 128 us -> 40.4 us (0.32)
  the two profiles are of different devices: /device:TPU:0 before, /device:TPU:24 now
where the time goes in v1:
time: 40.4 us; the launch traced here: 40.1 us
  Pallas kernels  34.2 us (85%)
  local copies, waits for them, and re-layouts  5.89 us (15%)
    pallas_call x1, Pallas kernels, on_device(): pl.pallas_call(functools.partial(kernel, count, reach), out_shape=jax.Sha...  34.2 us
    unnamed x11, local copies, waits for them, and re-layouts  5.89 us

profile of v1, /device:TPU:24, one launch (start us, length us, event | category | flops | bytes accessed | tf_op | source)
XLA Modules:
  0.0 40.1 jit_solution(2160243423284947331)
XLA Ops:
  0.0 0.0 copy-start
  0.0 1.9 %copy-done = bf16[3,2048,256]{2,1,0:T(8,128)(2,1)S(1)} copy-done((bf16[3,2048,256]{2,1,0:T(8,128)(2,1)S(1)}, bf16[3,2048,256]{2,1,0:T(8,128)(2,1)}, u32[]{:S(2)}) %copy-start) | copy-done | bytes 3145752
  1.9 0.0 copy-start.1
  1.9 0.9 %copy-done.1 = f32[3,3,2048]{2,1,0:T(4,128)S(1)} copy-done((f32[3,3,2048]{2,1,0:T(4,128)S(1)}, f32[3,3,2048]{2,1,0:T(4,128)}, u32[]{:S(2)}) %copy-start.1) | copy-done | bytes 73752
  2.8 0.0 copy-start.2
  2.8 0.8 %copy-done.2 = bf16[128,128]{1,0:T(8,128)(2,1)S(1)} copy-done((bf16[128,128]{1,0:T(8,128)(2,1)S(1)}, bf16[128,128]{1,0:T(8,128)(2,1)}, u32[]{:S(2)}) %copy-start.2) | copy-done | bytes 32792
  3.5 0.0 copy-start.3
  3.5 0.7 %copy-done.3 = f32[2048]{0:T(1024)S(1)} copy-done((f32[2048]{0:T(1024)S(1)}, f32[2048]{0:T(1024)}, u32[]{:S(2)}) %copy-start.3) | copy-done | bytes 8216
  4.2 0.0 copy-start.4
  4.2 0.7 %copy-done.4 = s32[256]{0:T(256)S(1)} copy-done((s32[256]{0:T(256)S(1)}, s32[256]{0:T(256)}, u32[]{:S(2)}) %copy-start.4) | copy-done | bytes 1048
  4.9 34.2 %shard_map.55 = bf16[2048,256]{1,0:T(8,128)(2,1)S(1)} custom-call(bf16[3,2048,256]{2,1,0:T(8,128)(2,1)S(1)} %copy-done, f32[3,3,2048]{2,1,0:T(4,128)S(1)} %copy-done.1, bf16[128,128]{1,0:T(8,128)(2,1)S(1)} %copy-done.2, f32[1,2048]{1,0:T(1,128)S(1)} %bitcast.2, s32[1,256]{1,0:T(1,128)S(1)} %bitcast.3), custom_call_target="tpu_custom_call" | custom-call | flops 1572864000 | bytes 4194304 | tf_op jit(solution)/shard_map/pallas_call | solution.py:266
  39.1 1.0 %copy.7 = bf16[2048,256]{1,0:T(8,128)(2,1)} copy(bf16[2048,256]{1,0:T(8,128)(2,1)S(1)} %shard_map.55) | data formatting | bytes 2097152
Async XLA Ops:
  0.0 1.9 %copy-start = (bf16[3,2048,256]{2,1,0:T(8,128)(2,1)S(1)}, bf16[3,2048,256]{2,1,0:T(8,128)(2,1)}, u32[]{:S(2)}) copy-start(bf16[3,2048,256]{2,1,0:T(8,128)(2,1)} %x_ref.1) | copy-start | bytes 9437188
  1.9 0.9 %copy-start.1 = (f32[3,3,2048]{2,1,0:T(4,128)S(1)}, f32[3,3,2048]{2,1,0:T(4,128)}, u32[]{:S(2)}) copy-start(f32[3,3,2048]{2,1,0:T(4,128)} %filt_ref.1) | copy-start | bytes 221188
  2.8 0.8 %copy-start.2 = (bf16[128,128]{1,0:T(8,128)(2,1)S(1)}, bf16[128,128]{1,0:T(8,128)(2,1)}, u32[]{:S(2)}) copy-start(bf16[128,128]{1,0:T(8,128)(2,1)} %mr_ref.1) | copy-start | bytes 98308
  3.5 0.7 %copy-start.3 = (f32[2048]{0:T(1024)S(1)}, f32[2048]{0:T(1024)}, u32[]{:S(2)}) copy-start(f32[2048]{0:T(1024)} %param.8) | copy-start | bytes 24580
  4.2 0.7 %copy-start.4 = (s32[256]{0:T(256)S(1)}, s32[256]{0:T(256)}, u32[]{:S(2)}) copy-start(s32[256]{0:T(256)} %param.9) | copy-start | bytes 3076

commit v2 on v1

--- a/solution.py
+++ b/solution.py
@@ -10,6 +10,9 @@
 NCAND = 4
 ROWS = 128
 LANES = 128
+AT_ONCE = 8
+PER = 2
+WIDE = PER * ROWS
 F32 = jnp.float32
 BF16 = jnp.bfloat16
 
@@ -32,8 +35,9 @@
 
 def kernel(
     count, reach,
-    x_ref, filt_ref, mr_ref, bias_ref, cand_ref, out_ref,
-    rows_ref, prm_ref, mrf_ref, shift_ref, band_ref, pool_ref, table_ref,
+    x_hbm, filt_hbm, mr_hbm, bias_hbm, cand_hbm, out_ref,
+    x_ref, filt_ref, mr_ref, bias_ref, cand_ref, load_sem,
+    rows_ref, prm_ref, mrf_ref, late_ref, early_ref, band_ref, pool_ref, table_ref,
     g0_ref, g1_ref, gh_ref, gate_ref, conv_ref, mixsum_ref,
     rim_out, rim_in, ids_in, sums_out, sums_in,
     halo_send, halo_recv, rim_send, rim_recv, ids_send, ids_recv, sums_send, sums_recv,
@@ -71,6 +75,11 @@
             send_sem=sums_send.at[d - 1], recv_sem=sums_recv.at[d - 1],
             device_id={"seq": me + d}, device_id_type=pl.DeviceIdType.MESH)
 
+    loads = [pltpu.make_async_copy(there, here, load_sem.at[i]) for i, (there, here) in enumerate((
+        (cand_hbm, cand_ref), (x_hbm, x_ref), (filt_hbm, filt_ref), (bias_hbm, bias_ref), (mr_hbm, mr_ref)))]
+    for load in loads:
+        load.start()
+
     def loop(low, high, body):
         def step(i, carry):
             body(i)
@@ -81,17 +90,38 @@
     loop(1, n_from + 1, lambda d: pl.semaphore_signal(
         barrier, inc=1, device_id={"seq": me - d}, device_id_type=pl.DeviceIdType.MESH))
 
+    loads[0].wait()
     own = cand_ref[...]
     start = earlier_ids(own, own)
     k2, t2 = iota((tokens, tokens), 0), iota((tokens, tokens), 1)
     inside = k2 >= start
     band_ref[...] = (inside & (k2 <= t2) & (t2 - k2 < LANES)).astype(F32).astype(BF16)
     pool_ref[...] = (inside & (k2 <= t2)).astype(F32).astype(BF16)
-    shift_ref[0] = (inside & (k2 == t2 - 1)).astype(F32).astype(BF16)
-    shift_ref[1] = (inside & (k2 == t2 - 2)).astype(F32).astype(BF16)
+    one = (inside & (k2 == t2 - 1)).astype(F32).astype(BF16)
+    two = (inside & (k2 == t2 - 2)).astype(F32).astype(BF16)
+    late_ref[...] = jnp.concatenate([one[:, LANES:], two[:, LANES:]], axis=1)
+    early_ref[...] = jnp.concatenate([one[:LANES, :LANES], two[:LANES, :LANES]], axis=1)
+
+    for load in loads[2:]:
+        load.wait()
+    rows_ref[...] = jnp.zeros_like(rows_ref)
+
+    def turn(i):
+        for u in range(PER):
+            rows = pl.ds(pl.multiple_of(i * WIDE + u * ROWS, ROWS), ROWS)
+            for j in range(3):
+                rows_ref[u, 3 * j:3 * j + 3, :] = filt_ref[j, :, rows]
+            rows_ref[u, 9:10, :] = bias_ref[:, rows]
+        for u in range(PER):
+            rows = pl.ds(pl.multiple_of(i * WIDE + u * ROWS, ROWS), ROWS)
+            prm_ref[rows, :] = rows_ref[u].T
+
+    loop(0, chunks // PER, turn)
+    mrf_ref[...] = mr_ref[...].astype(F32)
 
     row_k, lane_k = iota((16, LANES), 0), iota((16, LANES), 1)
     rim = jnp.zeros((16, channels), F32)
+    loads[1].wait()
     for b in range(3):
         pick = (lane_k - (LANES - 2) == row_k - 2 * b) & (lane_k >= LANES - 2)
         rim = rim + lax.dot_general(
@@ -109,31 +139,26 @@
     def _():
         rim_copy().start()
 
-    rows_ref[...] = jnp.zeros_like(rows_ref)
-
     def tail(i):
-        rows = pl.ds(pl.multiple_of(i * ROWS, ROWS), ROWS)
-        for j in range(3):
-            rows_ref[3 * j:3 * j + 3, :] = filt_ref[j, :, rows]
-        rows_ref[9:10, :] = bias_ref[:, rows]
-        prm = rows_ref[...].T
-        prm_ref[rows, :] = prm
-        outs = []
-        for b in (1, 2):
-            x = x_ref[b, rows, :]
-            one = dot(x, shift_ref[0, :, LANES:])
-            two = dot(x, shift_ref[1, :, LANES:])
-            outs.append(prm[:, b:b + 1] * x[:, LANES:].astype(F32)
-                        + prm[:, 3 + b:4 + b] * one + prm[:, 6 + b:7 + b] * two)
-        g1_ref[rows, :] = (outs[0] * outs[1]).astype(BF16)
+        many = [pl.ds(pl.multiple_of(i * WIDE + u * ROWS, ROWS), ROWS) for u in range(PER)]
+        x = [x_ref[b, rows, :] for rows in many for b in (1, 2)]
+        prm = [prm_ref[rows, :] for rows in many]
+        lags = dot(jnp.concatenate(x, axis=0), late_ref[...])
+        for u, rows in enumerate(many):
+            outs = []
+            for b in (1, 2):
+                at = 2 * u + b - 1
+                lag = lags[at * ROWS:(at + 1) * ROWS]
+                outs.append(prm[u][:, b:b + 1] * x[at][:, LANES:].astype(F32)
+                            + prm[u][:, 3 + b:4 + b] * lag[:, :LANES] + prm[u][:, 6 + b:7 + b] * lag[:, LANES:])
+            g1_ref[rows, :] = (outs[0] * outs[1]).astype(BF16)
 
         @pl.when(me + 1 < count)
         def _():
-            halo_copy(i).start()
-
-    loop(0, chunks, tail)
-    mrf_ref[...] = mr_ref[...].astype(F32)
-
+            for u in range(PER):
+                halo_copy(i * PER + u).start()
+
+    loop(0, chunks // PER, tail)
     @pl.when(me == 0)
     def _():
         gh_ref[...] = jnp.zeros_like(gh_ref)
@@ -155,44 +180,42 @@
         hit = (token == lane_q - lag) & (token >= start_all[:, :LANES]) & (token < 0) & (token >= -2)
         return hit.astype(F32).astype(BF16)
 
-    picks = [[rim_pick(b, lag) for lag in (1, 2)] for b in range(3)]
+    picks = [jnp.concatenate([rim_pick(b, 1), rim_pick(b, 2)], axis=1) for b in range(3)]
 
     def head(i):
-        rows = pl.ds(pl.multiple_of(i * ROWS, ROWS), ROWS)
-        prm = prm_ref[rows, :]
-        edge = rim_in[:, rows]
-        outs = []
-        for b in range(3):
-            x = x_ref[b, rows, :]
-            lags = [dot(x, shift_ref[j, :, :LANES]) + lax.dot_general(
-                edge, picks[b][j], (((0,), (0,)), ((), ())), preferred_element_type=F32)
-                for j in range(2)]
-            outs.append(prm[:, b:b + 1] * x[:, :LANES].astype(F32)
-                        + prm[:, 3 + b:4 + b] * lags[0] + prm[:, 6 + b:7 + b] * lags[1])
-        g0_ref[rows, :] = (outs[1] * outs[2]).astype(BF16)
-        gate_ref[rows, :LANES] = outs[0]
-        x = x_ref[0, rows, :]
-        one = dot(x, shift_ref[0, :, LANES:])
-        two = dot(x, shift_ref[1, :, LANES:])
-        gate_ref[rows, LANES:] = (prm[:, 0:1] * x[:, LANES:].astype(F32)
-                                  + prm[:, 3:4] * one + prm[:, 6:7] * two)
-
-    loop(0, chunks, head)
+        wide = pl.ds(pl.multiple_of(i * WIDE, WIDE), WIDE)
+        x = [x_ref[b, wide, :] for b in range(3)]
+        edge = rim_in[:, wide]
+        lags = [dot(x[b][:, :LANES], early_ref[...]) + lax.dot_general(
+            edge, picks[b], (((0,), (0,)), ((), ())), preferred_element_type=F32) for b in range(3)]
+        late = dot(x[0], late_ref[...])
+        prm = prm_ref[wide, :]
+
+        def short(b, now, lag):
+            return (prm[:, b:b + 1] * now.astype(F32)
+                    + prm[:, 3 + b:4 + b] * lag[:, :LANES] + prm[:, 6 + b:7 + b] * lag[:, LANES:])
+
+        g0_ref[wide, :] = (short(1, x[1][:, :LANES], lags[1]) * short(2, x[2][:, :LANES], lags[2])).astype(BF16)
+        gate_ref[wide, :LANES] = short(0, x[0][:, :LANES], lags[0])
+        gate_ref[wide, LANES:] = short(0, x[0][:, LANES:], late)
+
+    loop(0, chunks // PER, head)
 
     def conv(i):
-        for u in range(4):
-            group = i * 4 + u
-            rows = pl.ds(pl.multiple_of(group * size, size), size)
-            taps = jnp.broadcast_to(mrf_ref[pl.ds(group, 1), :], (LANES, LANES))
-            wheel = pltpu.roll(taps, 0, 1, stride=1, stride_axis=0).astype(BF16)
-            table_ref[group] = wheel * halo_mask
-            upper = jnp.concatenate([wheel, wheel], axis=1) * band_ref[:LANES, :]
-            right = wheel * band_ref[LANES:, LANES:]
-            near = dot(g0_ref[rows, :], upper)
-            conv_ref[rows, :LANES] = near[:, :LANES]
-            conv_ref[rows, LANES:] = near[:, LANES:] + dot(g1_ref[rows, :], right)
-
-    loop(0, groups // 4, conv)
+        some = [pl.ds(pl.multiple_of((i * AT_ONCE + u) * size, size), size) for u in range(AT_ONCE)]
+        near = [g0_ref[rows, :] for rows in some]
+        late = [g1_ref[rows, :] for rows in some]
+        taps = [mrf_ref[pl.ds(i * AT_ONCE + u, 1), :] for u in range(AT_ONCE)]
+        for u, rows in enumerate(some):
+            wheel = pltpu.roll(
+                jnp.broadcast_to(taps[u], (LANES, LANES)), 0, 1, stride=1, stride_axis=0).astype(BF16)
+            table_ref[i * AT_ONCE + u] = wheel * halo_mask
+            conv_ref[rows, :LANES] = dot(near[u], wheel * band_ref[:LANES, :LANES])
+            conv_ref[rows, LANES:] = dot(
+                jnp.concatenate([near[u], late[u]], axis=1),
+                jnp.concatenate([wheel, wheel], axis=0) * band_ref[:, LANES:])
+
+    loop(0, groups // AT_ONCE, conv)
 
     last = jnp.max(own.astype(F32), axis=1, keepdims=True)
     last_of = (iota((tokens, tokens), 0) >= earlier_ids(own, last.astype(jnp.int32)))
@@ -201,23 +224,26 @@
     mixsum_ref[...] = jnp.zeros_like(mixsum_ref)
 
     def mix(i):
-        rows = pl.ds(pl.multiple_of(i * ROWS, ROWS), ROWS)
-
         @pl.when(me > 0)
         def _():
-            halo_copy(i).wait_recv()
-
-        for u in range(per_chunk):
-            group = i * per_chunk + u
-            some = pl.ds(pl.multiple_of(group * size, size), size)
-            conv_ref[some, :LANES] += dot(gh_ref[some, :], table_ref[group])
-        bias = prm_ref[rows, 9:10]
-        gated = jnp.concatenate([g0_ref[rows, :], g1_ref[rows, :]], axis=1).astype(F32)
-        mixed = (gate_ref[rows, :] * (conv_ref[rows, :] + bias * gated)).astype(BF16)
-        conv_ref[rows, :] = dot(mixed, pool_ref[...])
-        mixsum_ref[...] += dot(mixed, jnp.where(lane_p == i, last_col, 0.0).astype(BF16))
-
-    loop(0, chunks, mix)
+            for u in range(PER):
+                halo_copy(i * PER + u).wait_recv()
+
+        wide = pl.ds(pl.multiple_of(i * WIDE, WIDE), WIDE)
+        far = [dot(gh_ref[pl.ds(pl.multiple_of(i * WIDE + u * size, size), size), :], table_ref[i * (WIDE // size) + u])
+               for u in range(WIDE // size)]
+        bias = prm_ref[wide, 9:10]
+        mixed = jnp.concatenate([
+            (gate_ref[wide, :LANES] * (conv_ref[wide, :LANES] + jnp.concatenate(far, axis=0)
+                                       + bias * g0_ref[wide, :].astype(F32))).astype(BF16),
+            (gate_ref[wide, LANES:] * (conv_ref[wide, LANES:] + bias * g1_ref[wide, :].astype(F32))).astype(BF16),
+        ], axis=1)
+        conv_ref[wide, :] = dot(mixed, pool_ref[...])
+        mixsum_ref[...] += sum(
+            dot(mixed[u * ROWS:(u + 1) * ROWS], jnp.where(lane_p == i * PER + u, last_col, 0.0).astype(BF16))
+            for u in range(PER))
+
+    loop(0, chunks // PER, mix)
 
     sums_out[...] = mixsum_ref[...].T[:sums_out.shape[0], :]
     loop(1, n_to + 1, lambda d: sums_copy(d).start())
@@ -266,13 +292,20 @@
     return pl.pallas_call(
         functools.partial(kernel, count, reach),
         out_shape=jax.ShapeDtypeStruct((channels, tokens), BF16),
-        in_specs=[vmem] * 5,
+        in_specs=[pl.BlockSpec(memory_space=pltpu.HBM)] * 5,
         out_specs=vmem,
         scratch_shapes=[
-            pltpu.VMEM((ROWS, LANES), F32),
+            pltpu.VMEM(features.shape, BF16),
+            pltpu.VMEM(short_filter.shape, F32),
+            pltpu.VMEM(mr_filter.shape, BF16),
+            pltpu.VMEM((1, channels), F32),
+            pltpu.VMEM((1, tokens), jnp.int32),
+            dma((5,)),
+            pltpu.VMEM((PER, ROWS, LANES), F32),
             pltpu.VMEM((channels, LANES), F32),
             pltpu.VMEM((groups, LANES), F32),
-            pltpu.VMEM((2, tokens, tokens), BF16),
+            pltpu.VMEM((tokens, tokens), BF16),
+            pltpu.VMEM((LANES, tokens), BF16),
             pltpu.VMEM((tokens, tokens), BF16),
             pltpu.VMEM((tokens, tokens), BF16),
             pltpu.VMEM((groups, LANES, LANES), BF16),
@@ -291,7 +324,7 @@
             dma((reach,)), dma((reach,)), dma((reach,)), dma((reach,)),
         ],
         compiler_params=pltpu.CompilerParams(
-            collective_id=0, has_side_effects=True, vmem_limit_bytes=48 << 20),
+            collective_id=0, has_side_effects=True, vmem_limit_bytes=60 << 20),
         cost_estimate=pl.CostEstimate(
             flops=2 * channels * tokens * 1500, bytes_accessed=8 * channels * tokens, transcendentals=0),
     )(features, short_filter, mr_filter, mr_bias[None, :], candidate[None, :])

time: 40.4 us -> 28.5 us (0.71)
  Pallas kernels: 34.2 us -> 26 us
  local copies, waits for them, and re-layouts: 5.89 us -> 2.26 us
    pallas_call x1, Pallas kernels: 34.2 us -> 26 us  [on_device(): pl.pallas_call(functools.partial(kernel, count, reach), out_shape=jax.Sha...]
    unnamed x11 -> x1, local copies, waits for them, and re-layouts: 5.89 us -> 2.26 us
where the time goes in v2:
time: 28.5 us; the launch traced here: 28.2 us
  Pallas kernels  26 us (91%)
  local copies, waits for them, and re-layouts  2.26 us (8%)
    pallas_call x1, Pallas kernels, on_device(): pl.pallas_call(functools.partial(kernel, count, reach), out_shape=jax.Sha...  26 us
    unnamed x1, local copies, waits for them, and re-layouts  2.26 us

profile of v2, /device:TPU:24, one launch (start us, length us, event | category | flops | bytes accessed | tf_op | source)
XLA Modules:
  0.0 28.2 jit_solution(17635491066855838515)
XLA Ops:
  0.0 26.0 %shard_map.55 = bf16[2048,256]{1,0:T(8,128)(2,1)} custom-call(bf16[3,2048,256]{2,1,0:T(8,128)(2,1)} %x_hbm.1, f32[3,3,2048]{2,1,0:T(4,128)} %filt_hbm.1, bf16[128,128]{1,0:T(8,128)(2,1)} %mr_hbm.1, f32[1,2048]{1,0:T(1,128)} %bitcast.2, s32[1,256]{1,0:T(1,128)} %bitcast.3), custom_call_target="tpu_custom_call" | custom-call | flops 1572864000 | bytes 4194304 | tf_op jit(solution)/shard_map/pallas_call | solution.py:292
  26.0 2.3 %copy.7 = bf16[2048,256]{1,0:T(8,128)(2,1)} copy(bf16[2048,256]{1,0:T(8,128)(2,1)} %shard_map.55) | data formatting | bytes 2097152

commit v3 on v2

--- a/solution.py
+++ b/solution.py
@@ -10,8 +10,8 @@
 NCAND = 4
 ROWS = 128
 LANES = 128
-AT_ONCE = 8
-PER = 2
+AT_ONCE = 16
+PER = 4
 WIDE = PER * ROWS
 F32 = jnp.float32
 BF16 = jnp.bfloat16
@@ -39,7 +39,7 @@
     x_ref, filt_ref, mr_ref, bias_ref, cand_ref, load_sem,
     rows_ref, prm_ref, mrf_ref, late_ref, early_ref, band_ref, pool_ref, table_ref,
     g0_ref, g1_ref, gh_ref, gate_ref, conv_ref, mixsum_ref,
-    rim_out, rim_in, ids_in, sums_out, sums_in,
+    rim_out, rim_in, picks_ref, ids_in, sums_out, sums_in,
     halo_send, halo_recv, rim_send, rim_recv, ids_send, ids_recv, sums_send, sums_recv,
 ):
     me = lax.axis_index("seq")
@@ -69,10 +69,10 @@
             send_sem=ids_send.at[d - 1], recv_sem=ids_recv.at[d - 1],
             device_id={"seq": me + d}, device_id_type=pl.DeviceIdType.MESH)
 
-    def sums_copy(d):
+    def sums_copy(d, half):
         return pltpu.make_async_remote_copy(
-            src_ref=sums_out, dst_ref=sums_in.at[d - 1],
-            send_sem=sums_send.at[d - 1], recv_sem=sums_recv.at[d - 1],
+            src_ref=sums_out.at[half], dst_ref=sums_in.at[d - 1, half],
+            send_sem=sums_send.at[d - 1, half], recv_sem=sums_recv.at[d - 1, half],
             device_id={"seq": me + d}, device_id_type=pl.DeviceIdType.MESH)
 
     loads = [pltpu.make_async_copy(there, here, load_sem.at[i]) for i, (there, here) in enumerate((
@@ -120,13 +120,15 @@
     mrf_ref[...] = mr_ref[...].astype(F32)
 
     row_k, lane_k = iota((16, LANES), 0), iota((16, LANES), 1)
-    rim = jnp.zeros((16, channels), F32)
+    rim = jnp.zeros((16, channels // 2), F32)
     loads[1].wait()
-    for b in range(3):
-        pick = (lane_k - (LANES - 2) == row_k - 2 * b) & (lane_k >= LANES - 2)
-        rim = rim + lax.dot_general(
-            pick.astype(F32).astype(BF16), x_ref[b, :, tokens - LANES:],
-            (((1,), (1,)), ((), ())), preferred_element_type=F32)
+    for half in range(2):
+        for b in range(3):
+            pick = (lane_k - (LANES - 2) == row_k - 8 * half - 2 * b) & (lane_k >= LANES - 2)
+            rim = rim + lax.dot_general(
+                pick.astype(F32).astype(BF16),
+                x_ref[b, half * channels // 2:(half + 1) * channels // 2, tokens - LANES:],
+                (((1,), (1,)), ((), ())), preferred_element_type=F32)
     rim_out[...] = rim.astype(BF16)
 
     @pl.when(me + 1 < count)
@@ -171,23 +173,36 @@
     loop(1, n_from + 1, lambda d: ids_copy(d).wait_recv())
 
     start_all = start + earlier_ids(ids_in[0][:, tokens - LANES:], own) - LANES
+    first = jnp.min(own.astype(F32), axis=1, keepdims=True).astype(jnp.int32)
+    before = lax.fori_loop(
+        1, n_from + 1,
+        lambda d, total: total + jnp.sum((ids_in[d - 1] == first).astype(F32), axis=1, keepdims=True),
+        jnp.zeros((1, 1), F32))
+    carried = (start == 0).astype(F32)
+    scale = 1.0 / jnp.sqrt((iota(start.shape, 1) + 1 - start).astype(F32) + carried * before)
+    carried = carried * scale
+
     kh, th = iota((LANES, LANES), 0), iota((LANES, LANES), 1)
     halo_mask = ((kh > th) & (kh - LANES >= start_all[:, :LANES])).astype(F32).astype(BF16)
     row_q, lane_q = iota((16, LANES), 0), iota((16, LANES), 1)
 
-    def rim_pick(b, lag):
-        token = row_q - 2 * b - 2
+    def rim_pick(half, b, lag):
+        token = row_q - 8 * half - 2 * b - 2
         hit = (token == lane_q - lag) & (token >= start_all[:, :LANES]) & (token < 0) & (token >= -2)
         return hit.astype(F32).astype(BF16)
 
-    picks = [jnp.concatenate([rim_pick(b, 1), rim_pick(b, 2)], axis=1) for b in range(3)]
+    for half in range(2):
+        for b in range(3):
+            picks_ref[half, b] = jnp.concatenate([rim_pick(half, b, 1), rim_pick(half, b, 2)], axis=1)
+    half_steps = chunks // PER // 2
 
     def head(i):
         wide = pl.ds(pl.multiple_of(i * WIDE, WIDE), WIDE)
         x = [x_ref[b, wide, :] for b in range(3)]
-        edge = rim_in[:, wide]
+        half = i // half_steps
+        edge = rim_in[:, pl.ds(pl.multiple_of((i - half * half_steps) * WIDE, WIDE), WIDE)]
         lags = [dot(x[b][:, :LANES], early_ref[...]) + lax.dot_general(
-            edge, picks[b], (((0,), (0,)), ((), ())), preferred_element_type=F32) for b in range(3)]
+            edge, picks_ref[half, b], (((0,), (0,)), ((), ())), preferred_element_type=F32) for b in range(3)]
         late = dot(x[0], late_ref[...])
         prm = prm_ref[wide, :]
 
@@ -217,10 +232,7 @@
 
     loop(0, groups // AT_ONCE, conv)
 
-    last = jnp.max(own.astype(F32), axis=1, keepdims=True)
-    last_of = (iota((tokens, tokens), 0) >= earlier_ids(own, last.astype(jnp.int32)))
-    last_col = last_of[:, :LANES].astype(F32)
-    lane_p = iota((tokens, LANES), 1)
+    lane_p = iota((ROWS, LANES), 1)
     mixsum_ref[...] = jnp.zeros_like(mixsum_ref)
 
     def mix(i):
@@ -238,40 +250,38 @@
                                        + bias * g0_ref[wide, :].astype(F32))).astype(BF16),
             (gate_ref[wide, LANES:] * (conv_ref[wide, LANES:] + bias * g1_ref[wide, :].astype(F32))).astype(BF16),
         ], axis=1)
-        conv_ref[wide, :] = dot(mixed, pool_ref[...])
-        mixsum_ref[...] += sum(
-            dot(mixed[u * ROWS:(u + 1) * ROWS], jnp.where(lane_p == i * PER + u, last_col, 0.0).astype(BF16))
-            for u in range(PER))
-
-    loop(0, chunks // PER, mix)
-
-    sums_out[...] = mixsum_ref[...].T[:sums_out.shape[0], :]
-    loop(1, n_to + 1, lambda d: sums_copy(d).start())
-
-    first = jnp.min(own.astype(F32), axis=1, keepdims=True).astype(jnp.int32)
+        local = dot(mixed, pool_ref[...])
+        conv_ref[wide, :] = local
+        half = i // half_steps
+        kept = mixsum_ref[half]
+        for u in range(PER):
+            kept = jnp.where(lane_p == (i - half * half_steps) * PER + u,
+                             local[u * ROWS:(u + 1) * ROWS, tokens - 1:], kept)
+        mixsum_ref[half] = kept
+
+    sum_rows = sums_out.shape[1]
+    for half in range(2):
+        loop(half * half_steps, (half + 1) * half_steps, mix)
+        sums_out[half] = mixsum_ref[half].T[:sum_rows, :]
+        loop(1, n_to + 1, lambda d: sums_copy(d, half).start())
+
+    here = chunks // 2
     mixsum_ref[...] = jnp.zeros_like(mixsum_ref)
-
-    def gather(d, before):
-        sums_copy(d).wait_recv()
-        ids = ids_in[d - 1]
-        same = jnp.max(ids.astype(F32), axis=1, keepdims=True).astype(jnp.int32) == first
-        mixsum_ref[:sums_out.shape[0], :] += jnp.where(same, sums_in[d - 1], 0.0)
-        return before + jnp.sum((ids == first).astype(F32), axis=1, keepdims=True)
-
-    before = lax.fori_loop(1, n_from + 1, gather, jnp.zeros((1, 1), F32))
-    carried = (start == 0).astype(F32)
-    seen = (iota(start.shape, 1) + 1 - start).astype(F32) + carried * before
-    scale = 1.0 / jnp.sqrt(seen)
-    mixsum_ref[...] = mixsum_ref[...].T
-
-    def finish(i):
-        rows = pl.ds(pl.multiple_of(i * ROWS, ROWS), ROWS)
-        column = jnp.sum(jnp.where(iota((ROWS, LANES), 1) == i, mixsum_ref[...], 0.0), axis=1, keepdims=True)
-        out_ref[rows, :] = ((conv_ref[rows, :] + column * carried) * scale).astype(BF16)
-
-    loop(0, chunks, finish)
-
-    loop(1, n_to + 1, lambda d: sums_copy(d).wait_send())
+    for half in range(2):
+
+        def gather(d):
+            sums_copy(d, half).wait_recv()
+            same = jnp.max(ids_in[d - 1].astype(F32), axis=1, keepdims=True).astype(jnp.int32) == first
+            mixsum_ref[half, :sum_rows, :] += jnp.where(same, sums_in[d - 1, half], 0.0)
+
+        loop(1, n_from + 1, gather)
+        columns = mixsum_ref[half].T
+        for i in range(here):
+            rows = pl.ds((half * here + i) * ROWS, ROWS)
+            out_ref[rows, :] = (conv_ref[rows, :] * scale + columns[:, i:i + 1] * carried).astype(BF16)
+
+    for half in range(2):
+        loop(1, n_to + 1, lambda d: sums_copy(d, half).wait_send())
     loop(1, n_to + 1, lambda d: ids_copy(d).wait_send())
 
     @pl.when(me + 1 < count)
@@ -286,7 +296,7 @@
     _, channels, tokens = features.shape
     groups = mr_filter.shape[0]
     chunks = channels // ROWS
-    sum_rows = -(-chunks // 8) * 8
+    sum_rows = -(-chunks // 16) * 8
     dma = pltpu.SemaphoreType.DMA
     vmem = pl.BlockSpec(memory_space=pltpu.VMEM)
     return pl.pallas_call(
@@ -314,14 +324,15 @@
             pltpu.VMEM((channels, LANES), BF16),
             pltpu.VMEM((channels, tokens), F32),
             pltpu.VMEM((channels, tokens), F32),
-            pltpu.VMEM((LANES, LANES), F32),
-            pltpu.VMEM((16, channels), BF16),
-            pltpu.VMEM((16, channels), BF16),
+            pltpu.VMEM((2, LANES, LANES), F32),
+            pltpu.VMEM((16, channels // 2), BF16),
+            pltpu.VMEM((16, channels // 2), BF16),
+            pltpu.VMEM((2, 3, 16, tokens), BF16),
             pltpu.VMEM((reach, 1, tokens), jnp.int32),
-            pltpu.VMEM((sum_rows, LANES), F32),
-            pltpu.VMEM((reach, sum_rows, LANES), F32),
+            pltpu.VMEM((2, sum_rows, LANES), F32),
+            pltpu.VMEM((reach, 2, sum_rows, LANES), F32),
             dma((chunks,)), dma((chunks,)), dma, dma,
-            dma((reach,)), dma((reach,)), dma((reach,)), dma((reach,)),
+            dma((reach,)), dma((reach,)), dma((reach, 2)), dma((reach, 2)),
         ],
         compiler_params=pltpu.CompilerParams(
             collective_id=0, has_side_effects=True, vmem_limit_bytes=60 << 20),

time: 28.5 us -> 25.3 us (0.89)
  Pallas kernels: 26 us -> 22.6 us
    pallas_call x1, Pallas kernels: 26 us -> 22.6 us  [on_device(): pl.pallas_call(functools.partial(kernel, count, reach), out_shape=jax.Sha...]
where the time goes in v3:
time: 25.3 us; the launch traced here: 24.9 us
  Pallas kernels  22.6 us (89%)
  local copies, waits for them, and re-layouts  2.26 us (9%)
    pallas_call x1, Pallas kernels, on_device(): pl.pallas_call(functools.partial(kernel, count, reach), out_shape=jax.Sha...  22.6 us
    unnamed x1, local copies, waits for them, and re-layouts  2.26 us

profile of v3, /device:TPU:24, one launch (start us, length us, event | category | flops | bytes accessed | tf_op | source)
XLA Modules:
  0.0 24.9 jit_solution(18028011080644812043)
XLA Ops:
  0.0 22.6 %shard_map.55 = bf16[2048,256]{1,0:T(8,128)(2,1)} custom-call(bf16[3,2048,256]{2,1,0:T(8,128)(2,1)} %x_hbm.1, f32[3,3,2048]{2,1,0:T(4,128)} %filt_hbm.1, bf16[128,128]{1,0:T(8,128)(2,1)} %mr_hbm.1, f32[1,2048]{1,0:T(1,128)} %bitcast.2, s32[1,256]{1,0:T(1,128)} %bitcast.3), custom_call_target="tpu_custom_call" | custom-call | flops 1572864000 | bytes 4194304 | tf_op jit(solution)/shard_map/pallas_call | solution.py:302
  22.6 2.3 %copy.7 = bf16[2048,256]{1,0:T(8,128)(2,1)} copy(bf16[2048,256]{1,0:T(8,128)(2,1)} %shard_map.55) | data formatting | bytes 2097152

commit v4 on v3

--- a/solution.py
+++ b/solution.py
@@ -77,8 +77,8 @@
 
     loads = [pltpu.make_async_copy(there, here, load_sem.at[i]) for i, (there, here) in enumerate((
         (cand_hbm, cand_ref), (x_hbm, x_ref), (filt_hbm, filt_ref), (bias_hbm, bias_ref), (mr_hbm, mr_ref)))]
-    for load in loads:
-        load.start()
+    for at in (0, 2, 3, 1, 4):
+        loads[at].start()
 
     def loop(low, high, body):
         def step(i, carry):
@@ -102,8 +102,8 @@
     late_ref[...] = jnp.concatenate([one[:, LANES:], two[:, LANES:]], axis=1)
     early_ref[...] = jnp.concatenate([one[:LANES, :LANES], two[:LANES, :LANES]], axis=1)
 
-    for load in loads[2:]:
-        load.wait()
+    loads[2].wait()
+    loads[3].wait()
     rows_ref[...] = jnp.zeros_like(rows_ref)
 
     def turn(i):
@@ -117,7 +117,6 @@
             prm_ref[rows, :] = rows_ref[u].T
 
     loop(0, chunks // PER, turn)
-    mrf_ref[...] = mr_ref[...].astype(F32)
 
     row_k, lane_k = iota((16, LANES), 0), iota((16, LANES), 1)
     rim = jnp.zeros((16, channels // 2), F32)
@@ -161,6 +160,9 @@
                 halo_copy(i * PER + u).start()
 
     loop(0, chunks // PER, tail)
+    loads[4].wait()
+    mrf_ref[...] = mr_ref[...].astype(F32)
+
     @pl.when(me == 0)
     def _():
         gh_ref[...] = jnp.zeros_like(gh_ref)

time: 25.3 us -> 24.7 us (0.976)
  Pallas kernels: 22.6 us -> 22.1 us
    pallas_call x1, Pallas kernels: 22.6 us -> 22.1 us  [on_device(): pl.pallas_call(functools.partial(kernel, count, reach), out_shape=jax.Sha...]
where the time goes in v4:
time: 24.7 us; the launch traced here: 24.3 us
  Pallas kernels  22.1 us (89%)
  local copies, waits for them, and re-layouts  2.26 us (9%)
    pallas_call x1, Pallas kernels, on_device(): pl.pallas_call(functools.partial(kernel, count, reach), out_shape=jax.Sha...  22.1 us
    unnamed x1, local copies, waits for them, and re-layouts  2.26 us

profile of v4, /device:TPU:24, one launch (start us, length us, event | category | flops | bytes accessed | tf_op | source)
XLA Modules:
  0.0 24.3 jit_solution(18419765431665547191)
XLA Ops:
  0.0 22.1 %shard_map.55 = bf16[2048,256]{1,0:T(8,128)(2,1)} custom-call(bf16[3,2048,256]{2,1,0:T(8,128)(2,1)} %x_hbm.1, f32[3,3,2048]{2,1,0:T(4,128)} %filt_hbm.1, bf16[128,128]{1,0:T(8,128)(2,1)} %mr_hbm.1, f32[1,2048]{1,0:T(1,128)} %bitcast.2, s32[1,256]{1,0:T(1,128)} %bitcast.3), custom_call_target="tpu_custom_call" | custom-call | flops 1572864000 | bytes 4194304 | tf_op jit(solution)/shard_map/pallas_call | solution.py:304
  22.1 2.3 %copy.7 = bf16[2048,256]{1,0:T(8,128)(2,1)} copy(bf16[2048,256]{1,0:T(8,128)(2,1)} %shard_map.55) | data formatting | bytes 2097152
